TPU v7x, 32 devices: a whole 2x2x4 slice. The times are simulated.
32 devices in a mesh: section: 2 (over x), dp: 16 (over z, y, core).
Axes of the slice: x: 2, y: 2, z: 4, core: 2. Of those that a mesh axis runs over, the one named last changes fastest.
Arguments:
- boundary: bfloat16 [2, 64, 13, 13, 512], P('section', 'dp'), may hold values from -6 to 6
- weights: bfloat16 [2, 4608, 512], P('section'), may hold values from -0.09375 to 0.09375
- biases: float32 [2, 512], P('section'), may hold values from -3 to 3
- frame_video: int32 [64], P('dp'), may hold values from 0 to 63
- video_clips: int32 [64], replicated, may hold values from 1 to 25, as said below
Outputs:
- section_results: bfloat16 [2, 64, 13, 13, 512], P('section', 'dp')
- weight_grads: float32 [2, 4608, 512], P('section', 'dp')
- bias_grads: float32 [2, 512], P('section', 'dp')
Inputs may be any that keep to these rules, and one draw needn't show every extreme that they name: `video_clips`: each video's clip count.
All inputs are finite; a program needn't handle non-finite values.
Results may differ from a plain program's by a relative error of at most 0.006.
Values may be sent and summed in bfloat16 or wider, within the bound.
A program may use at most 128 MiB of HBM per device.

v0:
```python
import functools

import jax
import jax.numpy as jnp
from jax import lax
from jax.experimental import pallas as pl
from jax.experimental.pallas import tpu as pltpu
from jax.sharding import PartitionSpec as P

VMEM_LIMIT = 54 * 1024 * 1024
MESH = pl.DeviceIdType.MESH
F32 = jnp.float32
BF16 = jnp.bfloat16
SLOTS = 16
AHEAD = (0, 2, 4, 6, 8, 10, 12, 13)
BACK = (0, 2, 4, 6, 8, 10, 12, 13)
TERMS = {1: (0, 4), 3: (4, 8), 4: (8, 10)}
REST = 10
EARLY = {2: (0, 3, (0, 1))}
LATE = ((3, 8, (2, 3, 4)), (8, 13, (5, 6)))


def line_sizes(chips):
    sizes = []
    while chips > 1:
        size = 4 if chips % 4 == 0 else 2 if chips % 2 == 0 else chips
        sizes.append(size)
        chips //= size
    return tuple(sizes)


def dest_at(own, step, size):
    rights = size - 1 - own
    low = jnp.where(step < rights, size - 1 - step, step - rights)
    high = jnp.where(step < own, step, size - 1 - (step - own))
    return jnp.where(own < (size + 1) // 2, low, high)


class Plan:
    def __init__(self, frames, side, channels, dp_count):
        self.frames, self.side, self.channels, self.dp_count = frames, side, channels, dp_count
        self.group = SLOTS * frames
        self.cells = side * frames
        self.half = channels // 2
        self.chips = dp_count // 2
        self.lines = line_sizes(self.chips)
        self.rows = 9 * channels // self.chips
        self.mine = self.rows // 2
        levels = len(self.lines)
        inner_first = tuple(reversed(range(levels)))
        outer_first = tuple(range(levels))
        self.pieces = []
        for keeper in range(2):
            if self.mine % 96 == 0 and self.lines == (4, 2):
                sixteenths = self.mine // 16
                turned = sixteenths // 6
                part = (sixteenths - turned) // 2
                cuts = [(part, inner_first), (sixteenths - turned - part, inner_first), (turned, outer_first)]
                begin = 0
                for size, order in cuts:
                    self.pieces.append((keeper, begin, 16 * size, order))
                    begin += 16 * size
            else:
                self.pieces.append((keeper, 0, self.mine, inner_first))
        self.wire = BF16 if all(size % 16 == 0 and begin % 16 == 0 for _, begin, size, _ in self.pieces) else F32

    def slots(self, piece, stage):
        order = self.pieces[piece][3]
        count = 1
        for line in order[stage:]:
            count *= self.lines[line]
        return count

    def arrivals(self, piece, stage):
        size = self.lines[self.pieces[piece][3][stage]]
        after = self.slots(piece, stage) // size
        if size == 2:
            return after
        return size * after if stage == len(self.lines) - 1 else (size + 1) * after


def kernel(plan, *refs):
    (x_hbm, w_hbm, bias_hbm, video_hbm, clips_hbm, res, wout, bout,
     w, wt, xin, xs, ds, wd, xt, xc, do, grad, pre, other_pre, pad,
     sent, arrived, returned, bsum, scale, bias_ref, video_ref, clips_ref, bias_in) = refs[:30]
    rest = list(refs[30:])
    lines, pieces = plan.lines, plan.pieces
    levels = len(lines)

    def take(count):
        taken = rest[:count]
        del rest[:count]
        return taken

    out_bufs = [take(levels) for _ in pieces]
    in_bufs = [take(levels) for _ in pieces]
    sums = [take(levels) for _ in pieces]
    last_in = take(len(pieces))
    own_in = take(len(pieces))
    line_send, = take(1)
    line_recv = [take(levels) for _ in pieces]
    last_recv = take(len(pieces))
    (load_sem, wload_sem, small_sem, ahead_send, ahead_recv, back_send, back_recv, xc_send, xc_recv, do_send, do_recv,
     pre_sem,
     keep_send, keep_recv, bias_send, bias_recv, own_recv) = rest

    frames, side, ch, half = plan.frames, plan.side, plan.channels, plan.half
    group, cells = plan.group, plan.cells
    sec = lax.axis_index("section")
    me = lax.axis_index("dp")
    core = lax.rem(me, 2)
    coords, strides = [], []
    stride = plan.dp_count
    for size in lines:
        stride //= size
        strides.append(stride)
        coords.append(lax.rem(lax.div(me, stride), size))
    first = sec == 0
    across = (1 - sec, me)
    twin = (sec, me + 1 - 2 * core)
    aslant = (1 - sec, me + 1 - 2 * core)

    upside = coords[0] >= (lines[0] + 1) // 2

    def row(i):
        return jnp.where(upside, side - 1 - i, i)

    def tap(a):
        return jnp.where(upside, 2 - a, a)

    first_rows = 3

    def load_row(i):
        return pltpu.make_async_copy(x_hbm.at[0, row(i)], xin.at[i], load_sem.at[0 if i < first_rows else 1])

    def wait_rows(k):
        rows = xin.at[0:first_rows] if k == 0 else xin.at[first_rows:side]
        pltpu.make_async_copy(rows, rows, load_sem.at[k]).wait()

    def load_w(n, a):
        part = pl.ds(pl.multiple_of(3 * ch * tap(a), 3 * ch), 3 * ch)
        columns = slice(half * n, half * (n + 1))
        return pltpu.make_async_copy(
            w_hbm.at[0, part, columns], w.at[3 * ch * a : 3 * ch * (a + 1), columns], wload_sem.at[n, a])

    def load_small(k):
        source, to = ((bias_hbm, bias_ref), (video_hbm, video_ref), (clips_hbm, clips_ref))[k]
        return pltpu.make_async_copy(source, to, small_sem.at[k])

    for k in range(3):
        load_small(k).start()
    for i in range(first_rows):
        load_row(i).start()
    for n in range(2):
        for a in range(3):
            load_w(n, a).start()
    for i in range(first_rows, side):
        load_row(i).start()

    barrier = pltpu.get_barrier_semaphore()
    for device in (across, aslant, twin):
        pl.semaphore_signal(barrier, inc=1, device_id=device, device_id_type=MESH)
    greeted = 3
    for own, size, stride in zip(coords, lines, strides):
        for there, exists in ((me - stride, own > 0), (me + stride, own < size - 1)):
            @pl.when(exists)
            def _():
                for device in (there, there + 1 - 2 * core):
                    pl.semaphore_signal(barrier, inc=1, device_id=(sec, device), device_id_type=MESH)

            greeted = greeted + 2 * exists.astype(jnp.int32)

    for ref in (xs, ds):
        for i in (0, side + 1):
            ref[i] = jnp.zeros((group, 3 * ch), BF16)
    xt[:, 0 : 2 * group] = jnp.zeros((ch, 2 * group), BF16)
    xt[:, (side + 1) * 2 * group : (side + 2) * 2 * group] = jnp.zeros((ch, 2 * group), BF16)
    pad[...] = jnp.zeros_like(pad)
    bsum[...] = jnp.zeros_like(bsum)

    def spread(ref, begin, end, lane=0):
        lanes = slice(lane, lane + ref.shape[-1])
        for i in range(begin, end):
            pad[i * group : i * group + cells, lanes] = ref[i].astype(F32).reshape(cells, ref.shape[-1])
        return pad[begin * group : end * group, lanes]

    def gather(ref, begin, end, value, order=lambda i: i, columns=slice(0, ch)):
        for i in range(begin, end):
            at = (i - begin) * group
            part = value[at : at + cells, :].reshape(side, frames, value.shape[1])
            ref[order(i), :, :, columns] = part.astype(BF16)

    def rounded(v):
        ids = lax.broadcasted_iota(jnp.int32, v.shape, 0)
        return jnp.where(lax.rem(ids, group) < cells, v, 0.0).astype(BF16).astype(F32)

    def moved(v, slots):
        if slots:
            v = pltpu.roll(v, slots * frames % v.shape[0], 0)
        return v.astype(BF16).reshape(v.shape[0] // group, group, v.shape[1])

    def put_inputs(begin, end, v):
        for b in range(3):
            xs[begin + 1 : end + 1, :, b * ch : (b + 1) * ch] = moved(v, 1 - b)
        xc[begin:end, 0] = moved(v, 0)

    def put_deltas(begin, end, v, lane=0):
        for b in range(3):
            at = pl.multiple_of(b * ch + lane, 128)
            ds[begin + 1 : end + 1, :, pl.ds(at, v.shape[1])] = moved(v, b - 1)

    def put_halves(begin, end, which, v):
        for b in range(3):
            wd[begin:end, which, :, half * b : half * (b + 1)] = moved(v, b - 1)
        bsum[0:1, :] += jnp.sum(v, axis=0, keepdims=True)

    def product(source, factor, begin, end, sign, columns=slice(0, ch), ready=lambda a: None):
        count = (end - begin) * group
        total = jnp.zeros((count, columns.stop - columns.start), F32)
        for a in range(3):
            ready(a)
            at = begin + 1 + sign * (a - 1)
            total += jnp.dot(source[at : at + end - begin].reshape(count, 3 * ch), factor[3 * ch * a : 3 * ch * (a + 1), columns],
                             preferred_element_type=F32)
        return total

    def conv(begin, end, columns=slice(0, ch), ready=lambda a: None):
        return product(xs, w, begin, end, 1, columns, ready) + bias_ref[:, columns]

    def conv_back(begin, end):
        return product(ds, wt, begin, end, -1)

    def transpose_w(a):
        for k in range(3 * a, 3 * a + 3):
            at = slice(ch * k, ch * (k + 1))
            wt[at, :] = w[at, :].T

    def ahead(k, columns=slice(0, ch)):
        rows = pl.ds(AHEAD[k], AHEAD[k + 1] - AHEAD[k])
        return pltpu.make_async_remote_copy(
            src_ref=sent.at[rows, :, :, columns], dst_ref=arrived.at[rows, :, :, columns],
            send_sem=ahead_send.at[0], recv_sem=ahead_recv.at[k], device_id=across, device_id_type=MESH)

    def back(k, which):
        rows = pl.ds(BACK[k], BACK[k + 1] - BACK[k])
        lane = pl.multiple_of(half * (core if which == 0 else 1 - core), 128)
        return pltpu.make_async_remote_copy(
            src_ref=sent.at[rows, :, :, pl.ds(lane, half)], dst_ref=returned.at[which, rows],
            send_sem=back_send.at[0], recv_sem=back_recv.at[k],
            device_id=(across, aslant)[which], device_id_type=MESH)

    def share_inputs(k):
        rows = pl.ds(AHEAD[k], AHEAD[k + 1] - AHEAD[k])
        return pltpu.make_async_remote_copy(
            src_ref=xc.at[rows, 0], dst_ref=xc.at[rows, 1], send_sem=xc_send.at[0], recv_sem=xc_recv.at[0],
            device_id=twin, device_id_type=MESH)

    def share_pre():
        lane = pl.multiple_of(half * (1 - core), 128)
        return pltpu.make_async_remote_copy(
            src_ref=pre.at[:, pl.ds(lane, half)], dst_ref=other_pre, send_sem=pre_sem.at[0], recv_sem=pre_sem.at[1],
            device_id=twin, device_id_type=MESH)

    def share_deltas(k, begin, end, source):
        return pltpu.make_async_remote_copy(
            src_ref=source, dst_ref=do.at[begin:end],
            send_sem=do_send.at[0], recv_sem=do_recv.at[k], device_id=twin, device_id_type=MESH)

    def wait_deltas(k, begin, end):
        theirs = do.at[begin:end]
        pltpu.make_async_copy(theirs, theirs, do_recv.at[k]).wait()

    def other_deltas(begin, end):
        return do[begin:end].reshape((end - begin) * group, half).astype(F32)

    def transpose_inputs():
        theirs = xc.at[:, 1]
        pltpu.make_async_copy(theirs, theirs, xc_recv.at[0]).wait()
        for begin in range(0, side, 2):
            end = min(begin + 2, side)
            part = xc[begin:end].reshape((end - begin) * 2 * group, ch)
            xt[:, (begin + 1) * 2 * group : (end + 1) * 2 * group] = part.T

    def weight_term(a, begin, end, fresh=False):
        wide = 2 * group
        term = jnp.dot(xt[:, (begin + a) * wide : (end + a) * wide], wd[begin:end].reshape((end - begin) * wide, 3 * half),
                       preferred_element_type=F32)
        for b in range(3):
            at = pl.ds(pl.multiple_of(ch * (3 * tap(a) + b), ch), ch)
            part = term[:, half * b : half * (b + 1)]
            grad[at, :] = part if fresh else grad[at, :] + part

    def sigmoid(v):
        return 1.0 / (1.0 + jnp.exp(-v))

    for k in range(3):
        load_small(k).wait()

    def ahead_rows(k, columns=slice(0, ch), ready=lambda a: None):
        begin, end = AHEAD[k], AHEAD[k + 1]
        v = conv(begin, end, columns, ready)
        s = sigmoid(v)
        gather(sent, begin, end, v * s, columns=columns)
        pre[begin * group : end * group, columns] = s * (1.0 + v * (1.0 - s))

    @pl.when(first)
    def _():
        wait_rows(0)
        put_inputs(0, first_rows, spread(xin, 0, first_rows))
        ahead_rows(0, slice(0, half), lambda a: load_w(0, a).wait())

    @pl.when(jnp.logical_not(first))
    def _():
        ids = lax.rem(lax.broadcasted_iota(jnp.int32, (group, ch), 0), frames)
        per_row = jnp.zeros((group, ch), F32)
        for f in range(frames):
            clip = clips_ref[video_ref[f]].astype(F32)
            per_row = jnp.where(ids == f, 1.0 / jnp.full((1, ch), clip, F32), per_row)
        scale[...] = per_row
        wait_rows(0)

    pl.semaphore_wait(barrier, greeted)

    back_rows = list(zip(BACK, BACK[1:]))
    final = len(back_rows) - 1

    def returned_deltas(k):
        begin, end = back_rows[k]
        rows = slice(begin * group, end * group)
        both = returned.at[:, begin:end]
        pltpu.make_async_copy(both, both, back_recv.at[k]).wait()
        for which in range(2):
            if which == 0:
                factor = pre[rows, pl.ds(pl.multiple_of(half * core, 128), half)]
            else:
                factor = other_pre[rows, :]
            d = rounded(spread(returned.at[which], begin, end, half * which) * factor)
            put_halves(begin, end, which, d)
        use = [k in chunks for chunks in uses].index(True)
        share_deltas(use, begin, end, wd.at[begin:end, 1, :, half : 2 * half]).start()

    def own_deltas(k):
        begin, end = back_rows[k]
        own = wd[begin:end, 0, :, half : 2 * half].reshape((end - begin) * group, half)
        put_deltas(begin, end, own.astype(F32), half * core)

    uses = [part[2] for part in list(EARLY.values()) + list(LATE)]

    def input_grad(begin, end, chunks):
        wait_deltas(uses.index(chunks), back_rows[chunks[0]][0], back_rows[chunks[-1]][1])
        for k in chunks:
            own_deltas(k)
            put_deltas(*back_rows[k], other_deltas(*back_rows[k]), half * (1 - core))
        gather(res.at[0], begin, end, conv_back(begin, end), row)

    @pl.when(first)
    def _():
        ahead(0, slice(0, half)).start()
        ahead_rows(0, slice(half, ch), lambda a: load_w(1, a).wait())
        ahead(0, slice(half, ch)).start()
        wait_rows(1)
        share_inputs(0).start()
        low = first_rows
        for k in range(1, len(AHEAD) - 1):
            high = min(AHEAD[k + 1] + 1, side)
            if high > low:
                put_inputs(low, high, spread(xin, low, high))
                low = high
            ahead_rows(k)
            ahead(k).start()
            share_inputs(k).start()
        share_pre().start()
        for a in range(3):
            transpose_w(a)
        transpose_inputs()
        share_pre().wait_recv()

        for k in range(final):
            returned_deltas(k)
            if k in TERMS:
                for a in range(3):
                    weight_term(a, *TERMS[k], TERMS[k][0] == 0)
            if k in EARLY:
                input_grad(*EARLY[k])
        weight_term(2, REST, BACK[final])

    @pl.when(jnp.logical_not(first))
    def _():
        for a in range(3):
            load_w(0, a).wait()
            load_w(1, a).wait()
            transpose_w(a)
        wait_rows(1)
        rows_of = []
        done, next_back = 0, 0
        for k, (begin, end) in enumerate(zip(AHEAD, AHEAD[1:])):
            ahead(k).wait_recv()
            put_inputs(begin, end, spread(arrived, begin, end))
            share_inputs(k).start()
            top = side if end == side else end - 1
            v = conv(done, top)
            s = sigmoid(v)
            g = spread(xin, done, top).reshape(top - done, group, ch) * scale[...]
            d = rounded(g.reshape((top - done) * group, ch) * (s * (1.0 + v * (1.0 - s))))
            put_deltas(done, top, d)
            rows_of.append((done, top))
            begin, done = done, top
            while next_back < len(BACK) - 1 and (BACK[next_back + 1] < done or done == side):
                low, high = BACK[next_back], BACK[next_back + 1]
                gather(sent, low, high, conv_back(low, high))
                for which in range(2):
                    back(next_back, which).start()
                next_back += 1
            lane = pl.multiple_of(ch + half * (1 - core), 128)
            share_deltas(0, begin, done, ds.at[begin + 1 : done + 1, :, pl.ds(lane, half)]).start()
            lane = pl.multiple_of(ch + half * core, 128)
            own = ds[begin + 1 : done + 1, :, pl.ds(lane, half)]
            put_halves(begin, done, 0, own.reshape((done - begin) * group, half).astype(F32))
            gather(res.at[0], begin, done, v * s, row)
        transpose_inputs()
        wait_deltas(0, 0, side)
        for begin, end in rows_of:
            put_halves(begin, end, 1, other_deltas(begin, end))
        weight_term(2, 0, side, True)

    def rest_of_gradient(a):
        @pl.when(first)
        def _():
            if a == 1:
                returned_deltas(final)
            weight_term(a, REST, side)

        pl.when(jnp.logical_not(first))(lambda: weight_term(a, 0, side, True))

    def arrival_at(piece, stage, slot, side_at):
        size = lines[pieces[piece][3][stage]]
        after = plan.slots(piece, stage) // size
        if size == 2:
            return lax.rem(slot, after)
        own = lax.div(slot, after) == coords[pieces[piece][3][stage]]
        return jnp.where(jnp.logical_and(own, side_at == 1), size * after + lax.rem(slot, after), slot)

    def line_copy(piece, stage, slot, dest, final=False):
        keeper, _, size, order = pieces[piece]
        line = order[stage]
        right = dest > coords[line]
        side_at = jnp.where(right, 0, 1)
        to = me + jnp.where(right, strides[line], -strides[line])
        if final:
            to = to - core + keeper
            at = 0 if lines[line] == 2 else side_at
            target, sem = last_in[piece].at[at, core], last_recv[piece].at[at]
        else:
            there = dest == coords[line] + jnp.where(right, 1, -1)
            after = plan.slots(piece, stage) // lines[line]
            if lines[line] == 2:
                at = lax.rem(slot, after)
            else:
                second = jnp.logical_and(there, jnp.logical_not(right))
                at = jnp.where(second, lines[line] * after + lax.rem(slot, after), slot)
            target, sem = in_bufs[piece][stage].at[at], line_recv[piece][stage].at[at]
        return pltpu.make_async_remote_copy(
            src_ref=out_bufs[piece][stage].at[slot], dst_ref=target,
            send_sem=line_send.at[0], recv_sem=sem, device_id=(sec, to), device_id_type=MESH)

    def arrival(piece, stage, slot, side_at):
        at = arrival_at(piece, stage, slot, side_at)
        pltpu.make_async_remote_copy(
            src_ref=out_bufs[piece][stage].at[slot], dst_ref=in_bufs[piece][stage].at[at],
            send_sem=line_send.at[0], recv_sem=line_recv[piece][stage].at[at],
            device_id=twin, device_id_type=MESH).wait_recv()
        return in_bufs[piece][stage][at].astype(F32)

    def last_arrival(piece, side_at):
        at = 0 if lines[pieces[piece][3][levels - 1]] == 2 else side_at
        both = last_in[piece].at[at]
        pltpu.make_async_copy(both, both, last_recv[piece].at[at]).wait()
        return last_in[piece][at].astype(F32)

    def send_on(piece, stage, slot, dest):
        line = pieces[piece][3][stage]
        if stage < levels - 1:
            line_copy(piece, stage, slot, dest).start()
            return
        next_to = jnp.abs(dest - coords[line]) == 1

        @pl.when(next_to)
        def _():
            line_copy(piece, stage, slot, dest, True).start()

        @pl.when(jnp.logical_not(next_to))
        def _():
            line_copy(piece, stage, slot, dest).start()

    def leaf(piece, slot):
        keeper, begin, size, order = pieces[piece]
        left, chip = slot, 0
        for line in reversed(order):
            chip = chip + lax.rem(left, lines[line]) * (strides[line] // 2)
            left = lax.div(left, lines[line])
        at = chip * plan.rows + keeper * plan.mine + begin
        return grad[pl.ds(pl.multiple_of(at, 8), size), :]

    def dest_slot(piece, stage, rest_slot, step):
        line = pieces[piece][3][stage]
        dest = dest_at(coords[line], step, lines[line])
        after = plan.slots(piece, stage) // lines[line]
        return dest, dest * after + rest_slot

    def is_early(piece, stage):
        return stage == 0 and lines[pieces[piece][3][0]] == 2

    def own_copy(piece, slot):
        keeper, _, _, order = pieces[piece]
        line = order[0]
        to = me + jnp.where(coords[line] == 0, strides[line], -strides[line]) - core + keeper
        return pltpu.make_async_remote_copy(
            src_ref=out_bufs[piece][0].at[slot], dst_ref=own_in[piece].at[core],
            send_sem=line_send.at[0], recv_sem=own_recv.at[straight.index(piece)], device_id=(sec, to), device_id_type=MESH)

    def is_direct(piece):
        return levels == 2 and is_early(piece, 0)

    def early_send(piece, rest_slot, own_block=False):
        dest, slot = dest_slot(piece, 0, rest_slot, 0)
        out_bufs[piece][0][slot] = leaf(piece, slot).astype(plan.wire)
        if own_block:
            own_copy(piece, slot).start()
        else:
            send_on(piece, 0, slot, dest)

    def line_step(piece, stage, rest_slot, step):
        line = pieces[piece][3][stage]
        size, own = lines[line], coords[line]
        if step < size - 1 and is_early(piece, stage):
            return
        dest, slot = dest_slot(piece, stage, rest_slot, step)
        if stage == 0:
            value = leaf(piece, slot)
        elif step == size - 1 and is_direct(piece):
            value = leaf(piece, dest_slot(piece, 0, slot, 1)[1])
        else:
            value = summed(piece, stage - 1, slot)
        total = sums[piece][stage]
        if step < size - 1:
            right = dest > own
            upstream = jnp.logical_or(jnp.logical_and(right, own > 0), jnp.logical_and(jnp.logical_not(right), own < size - 1))

            @pl.when(upstream)
            def _():
                both = value + arrival(piece, stage, slot, jnp.where(right, 0, 1))
                out_bufs[piece][stage][slot] = both.astype(plan.wire)

            @pl.when(jnp.logical_not(upstream))
            def _():
                out_bufs[piece][stage][slot] = value.astype(plan.wire)

            send_on(piece, stage, slot, dest)
        else:
            total[...] = value
            if stage < levels - 1:
                @pl.when(own > 0)
                def _():
                    total[...] += arrival(piece, stage, slot, 0)

                @pl.when(own < size - 1)
                def _():
                    total[...] += arrival(piece, stage, slot, 1)

    pending = set()

    def summed(piece, stage, rest_slot):
        if (piece, stage) not in pending:
            for step in range(lines[pieces[piece][3][stage]]):
                line_step(piece, stage, rest_slot, step)
        return sums[piece][stage][...]

    def keep_copy(piece):
        keeper, begin, size, _ = pieces[piece]
        return pltpu.make_async_remote_copy(
            src_ref=sums[piece][levels - 1],
            dst_ref=wout.at[0, begin : begin + size, half * (1 - keeper) : half * (2 - keeper)],
            send_sem=keep_send.at[0], recv_sem=keep_recv.at[piece % (len(pieces) // 2)], device_id=twin, device_id_type=MESH)

    def keep(piece):
        keeper, begin, size, _ = pieces[piece]

        @pl.when(core == keeper)
        def _():
            wout[0, begin : begin + size, half * keeper : half * (keeper + 1)] = sums[piece][levels - 1][...]

        @pl.when(core != keeper)
        def _():
            keep_copy(piece).start()

    def finish(piece):
        keeper, begin, size, order = pieces[piece]
        line = order[levels - 1]
        own = coords[line]

        @pl.when(core == keeper)
        def _():
            keep_copy(piece).wait_recv()

            def add(side_at):
                both = last_arrival(piece, side_at)
                for columns in range(2):
                    wout[0, begin : begin + size, half * columns : half * (columns + 1)] += both[columns]

            pl.when(own > 0)(lambda: add(0))
            pl.when(own < lines[line] - 1)(lambda: add(1))
            if is_direct(piece):
                pltpu.make_async_copy(own_in[piece], own_in[piece], own_recv.at[straight.index(piece)]).wait()
                for columns in range(2):
                    arrived_part = own_in[piece][columns].astype(F32)
                    wout[0, begin : begin + size, half * columns : half * (columns + 1)] += arrived_part

    def bias_copy(line, right):
        way = 0 if right else 1
        return pltpu.make_async_remote_copy(
            src_ref=bias_in.at[line, 1 + way], dst_ref=bias_in.at[line, 3 + way],
            send_sem=bias_send.at[line, way], recv_sem=bias_recv.at[line, way],
            device_id=(sec, me + strides[line] * (1 if right else -1)), device_id_type=MESH)

    def bias_step(line, step):
        own, size = coords[line], lines[line]
        for right in (True, False):
            way = 0 if right else 1

            @pl.when(own == (step if right else size - 1 - step))
            def _():
                if step > 0:
                    bias_copy(line, right).wait_recv()
                    bias_in[line, 1 + way] = bias_in[line, 0] + bias_in[line, 3 + way]
                else:
                    bias_in[line, 1 + way] = bias_in[line, 0]
                bias_copy(line, right).start()

    def bias_end(line):
        own, size = coords[line], lines[line]
        total = bias_in.at[line + 1, 0]
        total[...] = bias_in[line, 0]
        for right in (True, False):
            way = 0 if right else 1
            exists = own > 0 if right else own < size - 1
            waited = jnp.logical_and(own > 0, own < size - 1)

            @pl.when(exists)
            def _():
                pl.when(jnp.logical_not(waited))(lambda: bias_copy(line, right).wait_recv())
                total[...] += bias_in[line, 3 + way]

        if line == levels - 1:
            bias_swap().start()

    def bias_swap():
        return pltpu.make_async_remote_copy(
            src_ref=bias_in.at[levels, 0], dst_ref=bias_in.at[levels, 1],
            send_sem=bias_send.at[levels, 0], recv_sem=bias_recv.at[levels, 0],
            device_id=twin, device_id_type=MESH)

    bias_work = []
    for line in range(levels):
        for step in range(lines[line] - 1):
            bias_work.append(functools.partial(bias_step, line, step))
        bias_work.append(functools.partial(bias_end, line))

    def some_bias(count=1):
        for work in bias_work[:count]:
            work()
        del bias_work[:count]

    straight = [p for p, piece in enumerate(pieces) if piece[3][0] == levels - 1]
    turned = [p for p in range(len(pieces)) if p not in straight]
    top = levels - 1
    steps = lines[pieces[0][3][top]]

    def early(step):
        def down(piece, stage, slot):
            if stage == 0:
                if is_early(piece, 0):
                    early_send(piece, slot, is_direct(piece) and step == steps - 1)
                return
            for inner in range(lines[pieces[piece][3][stage]]):
                down(piece, stage - 1, dest_slot(piece, stage, slot, inner)[1])

        for piece in straight:
            if levels == 1:
                if step == 0:
                    down(piece, 0, 0)
            else:
                down(piece, top - 1, dest_slot(piece, top, 0, step)[1])

    def turn(step):
        for piece in turned:
            order = pieces[piece][3]
            for outer in range(lines[order[1]]):
                dest, rest_slot = dest_slot(piece, 1, 0, outer)
                line_step(piece, 0, rest_slot, step)
                if step == lines[order[0]] - 1:
                    pending.add((piece, 0))
                    line_step(piece, 1, 0, outer)
                    pending.discard((piece, 0))
            if step == lines[order[0]] - 1:
                keep(piece)

    def go(step):
        for piece in straight:
            line_step(piece, top, 0, step)
            if step == steps - 1:
                keep(piece)

    direct = all(is_direct(piece) for piece in straight)
    turns = lines[pieces[turned[0]][3][0]] if turned else 0
    def late(k):
        pl.when(first)(lambda: input_grad(*LATE[k]))

    staged = levels > 1 and lines[0] >= 4
    ends = jnp.logical_or(coords[0] == 0, coords[0] == lines[0] - 1)
    if staged:
        early(0)
        if turned:
            pl.when(ends)(lambda: turn(0))
    rest_of_gradient(1)
    bias_in[0, 0] = bsum[...]
    some_bias()
    if staged:
        early(1)
    rest_of_gradient(0)
    for step in range(2 if staged else 0, steps - 1):
        early(step)
    if turned:
        if staged:
            pl.when(jnp.logical_not(ends))(lambda: turn(0))
        else:
            turn(0)
    some_bias()

    for step in range(max(steps, turns - 1)):
        if 1 <= step + 1 < turns:
            turn(step + 1)
        some_bias((1, 2)[step] if step < 2 else 0)
        if step == min(1, steps - 2):
            early(steps - 1)
            if direct:
                go(steps - 1)
        if step < steps - direct:
            go(step)
        if step == steps - 2:
            for k in range(len(LATE)):
                late(k)

    for n, piece in enumerate(turned + straight):
        if n == len(pieces) // 2:
            some_bias(len(bias_work))
        finish(piece)

    bias_swap().wait_recv()
    share = ch // plan.dp_count
    place = me * share
    own_half = (place >= half) == (core == 1)
    bias_row = jnp.where(own_half, bias_in[levels, 0], bias_in[levels, 1])
    bout[...] = pltpu.roll(bias_row, lax.rem(half - lax.rem(place, half), half), 1)[0:1, 0:share]

    def sent_all(ref, sem):
        pltpu.make_async_copy(ref, ref, sem).wait()

    bias_swap().wait_send()
    for line, size in enumerate(lines):
        pl.when(coords[line] < size - 1)(lambda: bias_copy(line, True).wait_send())
        pl.when(coords[line] > 0)(lambda: bias_copy(line, False).wait_send())
    sent_all(wout.at[0, :, 0:half], keep_send.at[0])
    total = 0
    for piece, (_, _, size, order) in enumerate(pieces):
        for stage in range(levels):
            count = plan.slots(piece, stage)
            total += (count - count // lines[order[stage]]) * size
    sent_all(grad.at[0 : total * jnp.dtype(plan.wire).itemsize // 4], line_send.at[0])
    sent_all(xc.at[:, 0], xc_send.at[0])
    sent_all(do, do_send.at[0])
    pl.when(first)(lambda: share_pre().wait_send())
    pl.when(first)(lambda: sent_all(sent, ahead_send.at[0]))
    pl.when(jnp.logical_not(first))(lambda: sent_all(sent, back_send.at[0]))


def body(boundary, weights, biases, frame_video, video_clips):
    boundary = jnp.transpose(boundary, (0, 2, 3, 1, 4))
    _, side, _, frames, ch = boundary.shape
    dp_count = lax.axis_size("dp")
    plan = Plan(frames, side, ch, dp_count)
    half, group = plan.half, plan.group
    vmem = lambda *shape, dtype=BF16: pltpu.VMEM(shape, dtype)
    dma = pltpu.SemaphoreType.DMA
    scratch = [
        vmem(9 * ch, ch),
        vmem(9 * ch, ch),
        vmem(side, side, frames, ch),
        vmem(side + 2, group, 3 * ch),
        vmem(side + 2, group, 3 * ch),
        vmem(side, 2, group, 3 * half),
        vmem(ch, (side + 2) * 2 * group),
        vmem(side, 2, group, ch),
        vmem(side, group, half),
        vmem(9 * ch, half, dtype=F32),
        vmem(side * group, ch, dtype=F32),
        vmem(side * group, half, dtype=F32),
        vmem(side * group, ch, dtype=F32),
        vmem(side, side, frames, ch),
        vmem(side, side, frames, ch),
        vmem(2, side, side, frames, half),
        vmem(8, half, dtype=F32),
        vmem(group, ch, dtype=F32),
        vmem(1, ch, dtype=F32),
        pltpu.SMEM(frame_video.shape, jnp.int32),
        pltpu.SMEM(video_clips.shape, jnp.int32),
        vmem(len(plan.lines) + 1, 5, 8, half, dtype=F32),
    ]
    levels = len(plan.lines)
    wire = plan.wire
    every = [(p, stage) for p in range(len(plan.pieces)) for stage in range(levels)]
    height = lambda p: plan.pieces[p][2]
    scratch += [vmem(plan.slots(p, stage), height(p), half, dtype=wire) for p, stage in every]
    scratch += [vmem(plan.arrivals(p, stage), height(p), half, dtype=wire) for p, stage in every]
    scratch += [vmem(height(p), half, dtype=F32) for p, _ in every]
    ends = [1 if plan.lines[order[-1]] == 2 else 2 for _, _, _, order in plan.pieces]
    scratch += [vmem(end, 2, height(p), half, dtype=wire) for p, end in enumerate(ends)]
    scratch += [vmem(2, height(p), half, dtype=wire) for p in range(len(plan.pieces))]
    scratch += [dma((1,))]
    scratch += [dma((plan.arrivals(p, stage),)) for p, stage in every]
    scratch += [dma((end,)) for end in ends]
    steps, backs = len(AHEAD) - 1, len(BACK) - 1
    keeps = len(plan.pieces) // 2
    shapes = [(2,), (2, 3), (3,), (1,), (steps,), (1,), (backs,), (1,), (1,), (1,), (len(EARLY) + len(LATE),), (2,), (1,), (keeps,)]
    scratch += [dma(shape) for shape in shapes]
    scratch += [dma((levels + 1, 2)) for _ in range(2)]
    scratch += [dma((len(plan.pieces),))]
    whole = pl.BlockSpec(memory_space=pltpu.VMEM)
    share = 9 * ch // dp_count
    operands = [
        pltpu.with_memory_space_constraint(operand, pltpu.HBM)
        for operand in (boundary, weights, biases, frame_video, video_clips)
    ]
    results, kernel_grad, bias_grad = pl.pallas_call(
        functools.partial(kernel, plan),
        out_shape=(
            pltpu.VMEM(boundary.shape, BF16),
            pltpu.VMEM((1, share, ch), F32),
            pltpu.VMEM((1, ch // dp_count), F32),
        ),
        in_specs=[pl.BlockSpec(memory_space=pltpu.HBM)] * 5,
        out_specs=(whole, whole, whole),
        scratch_shapes=scratch,
        compiler_params=pltpu.CompilerParams(
            collective_id=0, has_side_effects=True, vmem_limit_bytes=VMEM_LIMIT
        ),
    )(*operands)
    return jnp.transpose(results, (0, 3, 1, 2, 4)), kernel_grad, bias_grad


def solution(mesh):
    return jax.shard_map(
        body,
        mesh=mesh,
        in_specs=(
            P("section", "dp", None, None, None),
            P("section", None, None),
            P("section", None),
            P("dp"),
            P(),
        ),
        out_specs=(
            P("section", "dp", None, None, None),
            P("section", "dp", None),
            P("section", "dp"),
        ),
        check_vma=False,
    )
```

profile of v0, /device:TPU:0, one launch (start us, length us, event | category | flops | bytes accessed | tf_op | source)
XLA Modules:
  0.0 58.7 jit_solution(5274904638830005963)
XLA Ops:
  0.6 55.9 %shard_map.76 = (bf16[1,13,13,4,512]{4,3,2,1,0:T(4,128)(2,1)S(1)}, f32[1,288,512]{2,1,0:T(8,128)S(1)}, f32[1,32]{1,0:T(1,128)S(1)}) custom-call(bf16[1,13,13,4,512]{4,3,2,1,0:T(4,128)(2,1)} %bitcast.3, bf16[1,4608,512]{2,1,0:T(8,128)(2,1)} %refs_1_.1, f32[1,512]{1,0:T(1,128)} %refs_2_.1, s32[4]{0:T(128)} %refs_3_.1, s32[64]{0:T(128)} %refs_4_.1), custom_call_target="tpu_custom_call" | custom-call | tf_op jit(solution)/shard_map/pallas_call | solution.py:843
  56.5 0.9 %copy.11 = bf16[1,4,13,13,512]{4,1,3,2,0:T(4,128)(2,1)} copy(bf16[1,4,13,13,512]{4,1,3,2,0:T(4,128)(2,1)S(1)} %bitcast.2) | data formatting | bytes 1384448
  57.4 0.5 copy.13
  57.9 0.8 %copy.12 = f32[1,288,512]{2,1,0:T(8,128)} copy(f32[1,288,512]{2,1,0:T(8,128)S(1)} %get-tuple-element.10) | data formatting | bytes 1179648
where the time goes:
time: 58.9 us; the launch traced here: 58.7 us
  Pallas kernels  55.9 us (95%)
  local copies, waits for them, and re-layouts  2.18 us (4%)
  between operations  0.64 us (1%)
    pallas_call x1, Pallas kernels, body(): pl.pallas_call(functools.partial(kernel, plan), out_shape=(pltpu.VMEM(bou...  55.9 us
    unnamed x3, local copies, waits for them, and re-layouts  2.18 us

commit v1 on v0

--- a/solution.py
+++ b/solution.py
@@ -408,7 +408,7 @@
             while next_back < len(BACK) - 1 and (BACK[next_back + 1] < done or done == side):
                 low, high = BACK[next_back], BACK[next_back + 1]
                 gather(sent, low, high, conv_back(low, high))
-                for which in range(2):
+                for which in (1, 0):
                     back(next_back, which).start()
                 next_back += 1
             lane = pl.multiple_of(ch + half * (1 - core), 128)

time: 58.9 us -> 58.8 us (level)
  no operation moved by 1% of the time
where the time goes in v1:
time: 58.8 us; the launch traced here: 58.4 us
  Pallas kernels  55.6 us (95%)
  local copies, waits for them, and re-layouts  2.18 us (4%)
  between operations  0.64 us (1%)
    pallas_call x1, Pallas kernels, body(): pl.pallas_call(functools.partial(kernel, plan), out_shape=(pltpu.VMEM(bou...  55.6 us
    unnamed x3, local copies, waits for them, and re-layouts  2.18 us

profile of v1, /device:TPU:0, one launch (start us, length us, event | category | flops | bytes accessed | tf_op | source)
XLA Modules:
  0.0 58.4 jit_solution(590699244396977459)
XLA Ops:
  0.6 55.6 %shard_map.76 = (bf16[1,13,13,4,512]{4,3,2,1,0:T(4,128)(2,1)S(1)}, f32[1,288,512]{2,1,0:T(8,128)S(1)}, f32[1,32]{1,0:T(1,128)S(1)}) custom-call(bf16[1,13,13,4,512]{4,3,2,1,0:T(4,128)(2,1)} %bitcast.3, bf16[1,4608,512]{2,1,0:T(8,128)(2,1)} %refs_1_.1, f32[1,512]{1,0:T(1,128)} %refs_2_.1, s32[4]{0:T(128)} %refs_3_.1, s32[64]{0:T(128)} %refs_4_.1), custom_call_target="tpu_custom_call" | custom-call | tf_op jit(solution)/shard_map/pallas_call | solution.py:843
  56.2 0.9 %copy.11 = bf16[1,4,13,13,512]{4,1,3,2,0:T(4,128)(2,1)} copy(bf16[1,4,13,13,512]{4,1,3,2,0:T(4,128)(2,1)S(1)} %bitcast.2) | data formatting | bytes 1384448
  57.0 0.5 copy.13
  57.6 0.8 %copy.12 = f32[1,288,512]{2,1,0:T(8,128)} copy(f32[1,288,512]{2,1,0:T(8,128)S(1)} %get-tuple-element.10) | data formatting | bytes 1179648
